TPU v7x, 128 devices: a whole 4x4x4 slice. The times are simulated.
128 devices in a mesh: dp: 4 (over y_hi, core), owner: 32 (over z, y_lo, x).
Axes of the slice: x: 4, y: 4 (y_hi: 2, y_lo: 2; y = y_hi * 2 + y_lo), z: 4, core: 2. Of those that a mesh axis runs over, the one named last changes fastest.
Arguments:
- stats: bfloat16 [32, 2, 8192, 768], P('owner', None, 'dp'), may hold values from -6 to 6
- damping: float32 [32, 2], P('owner'), may hold values from 0.1 to 1
- grad: bfloat16 [32, 768, 4, 768], P('owner', 'dp'), may hold values from -6 to 6
Outputs:
- precond: bfloat16 [32, 768, 4, 768], P('owner', 'dp')
All inputs are finite; a program needn't handle non-finite values. Where the computation divides by a largest or mean magnitude, that divisor is 1e-20 or more.
Results may differ from a plain program's by a relative error of at most 0.0063.
Values may be sent and summed in bfloat16 or wider, within the bound.
A program may use at most 128 MiB of HBM per device.

v0:
```python
import jax
import jax.numpy as jnp
from jax import lax
from jax.sharding import PartitionSpec as P

ITERS = 5


HIGH = lax.Precision.HIGHEST


def passed_along(block, axis, distance):
    devices = range(lax.axis_size(axis))
    route = [((i - distance) % len(devices), i) for i in devices]
    return lax.ppermute(block, axis, route)


def per_device(stats, damping, grad):
    groups = lax.axis_size("dp")
    group_idx = lax.axis_index("dp")
    width = stats.shape[3]
    total_tokens = stats.shape[2] * groups
    kind = group_idx // 2
    half = group_idx % 2
    half_rows = width // 2
    partial_cov = lax.dot_general(
        stats[0], stats[0], (((1,), (1,)), ((0,), (0,))), preferred_element_type=jnp.float32
    )
    summed = lax.psum(partial_cov, "dp")
    block_cov = lax.dynamic_index_in_dim(summed, kind, 0, keepdims=False)
    block_cov = block_cov / total_tokens
    lam = lax.dynamic_index_in_dim(damping[0], kind, 0, keepdims=False)
    eye = jnp.eye(width, dtype=jnp.float32)
    matrix = block_cov + lam * eye
    factor = 1.0 / jnp.max(jnp.sum(jnp.abs(matrix), axis=1))
    iterate = eye * factor
    for step in range(ITERS):
        product = jnp.dot(matrix, iterate, precision=HIGH, preferred_element_type=jnp.float32)
        iterate = 2.0 * iterate - jnp.dot(
            iterate, product, precision=HIGH, preferred_element_type=jnp.float32
        )
    row_part = lax.dynamic_slice_in_dim(iterate, half * half_rows, half_rows, 0)
    both_inv = lax.all_gather(row_part.astype(jnp.bfloat16), "dp", axis=0, tiled=True).reshape(
        2, width, width
    )
    a_inv = both_inv[0]
    g_inv = both_inv[1]
    tiles = grad[0]
    quarter = tiles.shape[0]
    band = tiles.shape[1]
    right_parts = [
        jnp.dot(tiles[:, 0, :], a_inv, preferred_element_type=jnp.float32).astype(jnp.bfloat16)
    ]
    for offset in range(1, band):
        column_inv = passed_along(a_inv, "owner", offset)
        right_parts.append(
            jnp.dot(tiles[:, offset, :], column_inv, preferred_element_type=jnp.float32).astype(
                jnp.bfloat16
            )
        )
    right_flat = jnp.stack(right_parts, axis=1).reshape(quarter, band * width)
    own_left = lax.dynamic_slice_in_dim(g_inv, group_idx * quarter, quarter, 0)
    summed_rows = jnp.dot(
        own_left,
        lax.all_gather(right_flat, "dp", axis=0, tiled=True),
        preferred_element_type=jnp.float32,
    )
    return summed_rows.astype(jnp.bfloat16).reshape(1, quarter, band, width)


def solution(mesh):
    in_specs = (P("owner", None, "dp", None), P("owner", None), P("owner", "dp", None, None))
    out_specs = P("owner", "dp", None, None)
    return jax.shard_map(
        per_device, mesh=mesh, in_specs=in_specs, out_specs=out_specs, check_vma=False
    )
```

profile of v0, /device:TPU:1, one launch (start us, length us, event | category | flops | bytes accessed | tf_op | source)
XLA Modules:
  0.0 356.4 jit_solution(2121340063414853971)
XLA Ops:
  6.5 10.6 %fusion = f32[2,768,768]{2,1,0:T(8,128)} fusion(bf16[1,2,2048,768]{3,2,1,0:T(8,128)(2,1)} %param.3), kind=kOutput, calls=%fused_computation | convolution fusion | flops 4831838208 | bytes 11010048 | tf_op jit(solution)/shard_map/dot_general | solution.py:26
  18.0 104.4 %all-reduce.2.cloned.1.call-done = f32[2,768,768]{2,1,0:T(8,128)} async-done(((f32[2,768,768]{2,1,0:T(8,128)}), f32[2,768,768]{2,1,0:T(8,128)}) %all-reduce.2.cloned.1.call-update) | async-done | bytes 4718608 | tf_op jit(solution)/shard_map/psum | solution.py:29
  122.4 2.7 abs_reduce_fusion
  126.3 8.3 %fusion.4 = f32[768,768]{1,0:T(8,128)S(1)} fusion(f32[]{:T(128)S(6)} %div.25, f32[2,768,768]{2,1,0:T(8,128)} %all-reduce.2.cloned.1.call-done, s32[]{:T(128)S(6)} %select_n.24, f32[]{:T(128)} %bitcast.2), kind=kOutput, calls=%fused_computation.4 | convolution fusion | flops 5439356928 | bytes 4719112 | tf_op jit(solution)/shard_map/dot_general | solution.py:38
  134.6 5.8 %fusion.6 = f32[768,768]{1,0:T(8,128)S(1)} fusion(f32[768,768]{1,0:T(8,128)S(1)} %fusion.4, f32[]{:T(128)S(6)} %div.25), kind=kOutput, calls=%fused_computation.8 | convolution fusion | flops 5439356928 | bytes 4718596 | tf_op jit(solution)/shard_map/dot_general | solution.py:39
  140.4 6.9 %fusion.26 = f32[768,768]{1,0:T(8,128)S(1)} fusion(f32[768,768]{1,0:T(8,128)S(1)} %fusion.6, f32[2,768,768]{2,1,0:T(8,128)S(1)} %bitcast.65, s32[]{:T(128)S(6)} %select_n.24, f32[]{:T(128)} %bitcast.2), kind=kOutput, calls=%fused_computation.45 | convolution fusion | flops 5438177280 | bytes 7077896 | tf_op jit(solution)/shard_map/dot_general | solution.py:38
  147.3 6.1 %multiply_subtract_fusion.2 = f32[768,768]{1,0:T(8,128)S(1)} fusion(f32[768,768]{1,0:T(8,128)S(1)} %fusion.6, f32[768,768]{1,0:T(8,128)S(1)} %fusion.26), kind=kOutput, calls=%fused_computation.12 | convolution fusion | flops 5436997632 | bytes 7077888 | tf_op jit(solution)/shard_map/dot_general | solution.py:39
  153.4 7.1 %fusion.25 = f32[768,768]{1,0:T(8,128)S(1)} fusion(f32[768,768]{1,0:T(8,128)S(1)} %multiply_subtract_fusion.2, f32[2,768,768]{2,1,0:T(8,128)S(1)} %bitcast.65, s32[]{:T(128)S(6)} %select_n.24, f32[]{:T(128)} %bitcast.2), kind=kOutput, calls=%fused_computation.44 | convolution fusion | flops 5438177280 | bytes 7077896 | tf_op jit(solution)/shard_map/dot_general | solution.py:38
  160.5 6.1 %multiply_subtract_fusion.1 = f32[768,768]{1,0:T(8,128)S(1)} fusion(f32[768,768]{1,0:T(8,128)S(1)} %multiply_subtract_fusion.2, f32[768,768]{1,0:T(8,128)S(1)} %fusion.25), kind=kOutput, calls=%fused_computation.11 | convolution fusion | flops 5436997632 | bytes 7077888 | tf_op jit(solution)/shard_map/dot_general | solution.py:39
  166.6 6.8 %fusion.24 = f32[768,768]{1,0:T(8,128)S(1)} fusion(f32[768,768]{1,0:T(8,128)S(1)} %multiply_subtract_fusion.1, f32[2,768,768]{2,1,0:T(8,128)S(1)} %bitcast.65, s32[]{:T(128)S(6)} %select_n.24, f32[]{:T(128)} %bitcast.2), kind=kOutput, calls=%fused_computation.43 | convolution fusion | flops 5438177280 | bytes 7077896 | tf_op jit(solution)/shard_map/dot_general | solution.py:38
  173.4 6.1 %multiply_subtract_fusion = f32[768,768]{1,0:T(8,128)S(1)} fusion(f32[768,768]{1,0:T(8,128)S(1)} %multiply_subtract_fusion.1, f32[768,768]{1,0:T(8,128)S(1)} %fusion.24), kind=kOutput, calls=%fused_computation.10 | convolution fusion | flops 5436997632 | bytes 7077888 | tf_op jit(solution)/shard_map/dot_general | solution.py:39
  179.5 6.7 %fusion.23 = f32[768,768]{1,0:T(8,128)S(1)} fusion(f32[768,768]{1,0:T(8,128)S(1)} %multiply_subtract_fusion, f32[2,768,768]{2,1,0:T(8,128)S(1)} %bitcast.65, s32[]{:T(128)S(6)} %select_n.24, f32[]{:T(128)} %bitcast.2), kind=kOutput, calls=%fused_computation.42 | convolution fusion | flops 5438177280 | bytes 7077896 | tf_op jit(solution)/shard_map/dot_general | solution.py:38
  186.2 6.2 %fusion.28 = f32[768,768]{1,0:T(8,128)S(1)} fusion(f32[768,768]{1,0:T(8,128)S(1)} %multiply_subtract_fusion, f32[768,768]{1,0:T(8,128)S(1)} %fusion.23), kind=kOutput, calls=%fused_computation.47 | convolution fusion | flops 5435817984 | bytes 7077888 | tf_op jit(solution)/shard_map/dot_general | solution.py:39
  193.5 27.6 %all-gather.3.cloned.1.call-done = bf16[1536,768]{1,0:T(8,128)(2,1)} async-done(((bf16[384,768]{1,0:T(8,128)(2,1)}), bf16[1536,768]{1,0:T(8,128)(2,1)}) %all-gather.3.cloned.1.call-update) | async-done | bytes 2359312 | tf_op jit(solution)/shard_map/all_gather | solution.py:43
  221.1 1.8 fusion.27
  222.9 1.3 collective-permute-start
  224.1 2.4 collective-permute-start.1
  226.5 1.2 collective-permute-start.2
  228.3 26.2 %collective-permute-done = bf16[768,768]{1,0:T(8,128)(2,1)S(1)} collective-permute-done((bf16[768,768]{1,0:T(8,128)(2,1)S(1)}, bf16[768,768]{1,0:T(8,128)(2,1)S(1)}, u32[]{:S(2)}, u32[]{:S(2)}) %collective-permute-start) | collective-permute-done | bytes 1179680 | tf_op jit(solution)/shard_map/ppermute | solution.py:15
  254.9 39.6 %collective-permute-done.1 = bf16[768,768]{1,0:T(8,128)(2,1)S(1)} collective-permute-done((bf16[768,768]{1,0:T(8,128)(2,1)S(1)}, bf16[768,768]{1,0:T(8,128)(2,1)S(1)}, u32[]{:S(2)}, u32[]{:S(2)}) %collective-permute-start.1) | collective-permute-done | bytes 1179680 | tf_op jit(solution)/shard_map/ppermute | solution.py:15
  294.8 9.8 %collective-permute-done.2 = bf16[768,768]{1,0:T(8,128)(2,1)S(1)} collective-permute-done((bf16[768,768]{1,0:T(8,128)(2,1)S(1)}, bf16[768,768]{1,0:T(8,128)(2,1)S(1)}, u32[]{:S(2)}, u32[]{:S(2)}) %collective-permute-start.2) | collective-permute-done | bytes 1179680 | tf_op jit(solution)/shard_map/ppermute | solution.py:15
  306.4 38.1 %all-gather.5.cloned.1.call-done = bf16[768,3072]{1,0:T(8,128)(2,1)} async-done(((bf16[192,3072]{1,0:T(8,128)(2,1)}), bf16[768,3072]{1,0:T(8,128)(2,1)}) %all-gather.5.cloned.1.call-update) | async-done | bytes 4718608 | tf_op jit(solution)/shard_map/all_gather | solution.py:65
  344.5 3.5 convolution_convert_fusion
  347.9 1.7 reshape.17
  (27 shorter events, 5.5 us)
Async XLA Ops:
  6.5 10.9 %copy-start = (f32[1,2]{1,0:T(1,128)S(1)}, f32[1,2]{1,0:T(1,128)}, u32[]{:S(2)}) copy-start(f32[1,2]{1,0:T(1,128)} %param.4) | copy-start | bytes 28
  6.5 115.9 %all-reduce.2.cloned.1.call-start = ((), (), s32[]{:S(2)}) async-start(), calls=%async_computation | async-start | bytes 9437184 | tf_op jit(solution)/shard_map/psum | solution.py:29
  17.2 203.9 %all-gather.3.cloned.1.call-start = ((), (), s32[]{:S(2)}) async-start(), calls=%async_computation.1 | async-start | bytes 2949120 | tf_op jit(solution)/shard_map/all_gather | solution.py:43
  122.4 18.0 %slice-start = ((s8[4718592]{0:T(1024)(128)(4,1)}), s8[524288]{0:T(1024)(128)(4,1)S(1)}, s32[]{:S(2)}) async-start(s8[4718592]{0:T(1024)(128)(4,1)} %bitcast.64), calls=%async_computation.3 | async-start | bytes 1048576
  126.3 14.1 %slice-start.1 = ((s8[4718592]{0:T(1024)(128)(4,1)}), s8[4194304]{0:T(1024)(128)(4,1)S(1)}, s32[]{:S(2)}) async-start(s8[4718592]{0:T(1024)(128)(4,1)} %bitcast.64), calls=%async_computation.4 | async-start | bytes 8388608
  193.4 34.3 %copy-start.2 = (bf16[1,192,4,768]{3,2,1,0:T(4,128)(2,1)S(1)}, bf16[1,192,4,768]{3,2,1,0:T(4,128)(2,1)}, u32[]{:S(2)}) copy-start(bf16[1,192,4,768]{3,2,1,0:T(4,128)(2,1)} %param.5) | copy-start | bytes 3538948
  193.4 151.0 %all-gather.5.cloned.1.call-start = ((), (), s32[]{:S(2)}) async-start(), calls=%async_computation.2 | async-start | bytes 5898240 | tf_op jit(solution)/shard_map/all_gather | solution.py:65
  222.9 5.0 %copy-start.1 = (bf16[1536,768]{1,0:T(8,128)(2,1)S(1)}, bf16[1536,768]{1,0:T(8,128)(2,1)}, u32[]{:S(2)}) copy-start(bf16[1536,768]{1,0:T(8,128)(2,1)} %all-gather.3.cloned.1.call-done) | copy-start | bytes 7077892
  222.9 31.6 %collective-permute-start = (bf16[768,768]{1,0:T(8,128)(2,1)S(1)}, bf16[768,768]{1,0:T(8,128)(2,1)S(1)}, u32[]{:S(2)}, u32[]{:S(2)}) collective-permute-start(bf16[768,768]{1,0:T(8,128)(2,1)S(1)} %get-tuple-element.6), channel_id=1, source_target_pairs={{31,0},{0,1},{1,2},{2,3},{3,4},{4,5},{5,6},{6,7},{7,8},{8,9},{9,10... | collective-permute-start | bytes 3538952 | tf_op jit(solution)/shard_map/ppermute | solution.py:15
  224.1 70.3 %collective-permute-start.1 = (bf16[768,768]{1,0:T(8,128)(2,1)S(1)}, bf16[768,768]{1,0:T(8,128)(2,1)S(1)}, u32[]{:S(2)}, u32[]{:S(2)}) collective-permute-start(bf16[768,768]{1,0:T(8,128)(2,1)S(1)} %get-tuple-element.6), channel_id=1, source_target_pairs={{30,0},{31,1},{0,2},{1,3},{2,4},{3,5},{4,6},{5,7},{6,8},{7,9},{8,1... | collective-permute-start | bytes 3538952 | tf_op jit(solution)/shard_map/ppermute | solution.py:15
  226.5 78.1 %collective-permute-start.2 = (bf16[768,768]{1,0:T(8,128)(2,1)S(1)}, bf16[768,768]{1,0:T(8,128)(2,1)S(1)}, u32[]{:S(2)}, u32[]{:S(2)}) collective-permute-start(bf16[768,768]{1,0:T(8,128)(2,1)S(1)} %get-tuple-element.6), channel_id=1, source_target_pairs={{29,0},{30,1},{31,2},{0,3},{1,4},{2,5},{3,6},{4,7},{5,8},{6,9},{7,... | collective-permute-start | bytes 3538952 | tf_op jit(solution)/shard_map/ppermute | solution.py:15
Sparse Core Ops, SparseCore 0:
  17.3 105.0 all-reduce.1
  193.6 27.4 all-gather.2
  306.5 37.9 all-gather.4
where the time goes:
time: 359 us; the launch traced here: 356 us
  waiting for transfers between devices  246 us (69%)
  matrix products  81.7 us (23%)
  between operations  14.2 us (4%)
  local copies, waits for them, and re-layouts  5.39 us (2%)
  starting transfers between devices  5.12 us (1%)
  other arithmetic  4.41 us (1%)
    psum x1, waiting for transfers between devices, per_device(): summed = lax.psum(partial_cov, 'dp')  104 us
    ppermute x3, waiting for transfers between devices, passed_along(): return lax.ppermute(block, axis, route)  75.5 us
    all_gather x1, waiting for transfers between devices, per_device(): lax.all_gather(right_flat, 'dp', axis=0, tiled=True)  38.1 us
    dot_general x5, matrix products, per_device(): jnp.dot(matrix, iterate, precision=HIGH, preferred_element_type=jnp.float32)  35.8 us
    dot_general x5, matrix products, per_device(): jnp.dot(iterate, product, precision=HIGH, preferred_element_type=jnp.floa...  30.3 us
    all_gather x1, waiting for transfers between devices, per_device(): lax.all_gather(row_part.astype(jnp.bfloat16), 'dp', axis=0, tiled=True)  27.6 us
    dot_general x1, matrix products, per_device(): lax.dot_general(stats[0], stats[0], (((1,), (1,)), ((0,), (0,))), preferr...  10.6 us
  transfers between devices with their start and end apart: 6, of which 6 were waited for; matrix products, arithmetic and copies ran while one was open for 1% of the time, Pallas kernels for 0%

commit v1 on v0

v1 whole, which is shorter than its diff:
```python
import jax
import jax.numpy as jnp
from jax import lax
from jax.experimental import pallas as pl
from jax.experimental.pallas import tpu as pltpu
from jax.sharding import PartitionSpec as P

MESH = pl.DeviceIdType.MESH
F32 = jnp.float32
BF16 = jnp.bfloat16
N = 256
W = 768
PAIRS = ((0, 0), (0, 1), (0, 2), (1, 1), (1, 2), (2, 2))
TAIL = len(PAIRS) * N
ROWS = TAIL + 16
CHUNKS = ((0, 512), (512, 512), (1024, 528))
CHUNK_PAIRS = ((0, 1), (2, 3), (4, 5))
TOKEN_CHUNK = 1024


def eye_mask():
    shape = (N, N)
    return lax.broadcasted_iota(jnp.int32, shape, 0) == lax.broadcasted_iota(jnp.int32, shape, 1)


def gram(a, b):
    return lax.dot_general(a, b, (((0,), (0,)), ((), ())), preferred_element_type=F32)


def pack_diagonal(diags):
    row = lax.broadcasted_iota(jnp.int32, (16, N), 0)
    out = jnp.zeros((16, N), F32)
    for i, d in enumerate(diags):
        high = d.astype(BF16).astype(F32)
        out = jnp.where(row == i, high, out)
        out = jnp.where(row == i + 3, d - high, out)
    return out.astype(BF16)


def unpack_diagonal(tail):
    t = tail.astype(F32)
    return [t[i : i + 1] + t[i + 3 : i + 4] for i in range(3)]


def invert(packed, tokens, off_r, off_s, r_mat, s_mat, result):
    eye = eye_mask()
    diag = [d * (1.0 / tokens) for d in unpack_diagonal(packed[TAIL:ROWS, :])]
    sums = [None] * 3

    def add(i, v):
        sums[i] = v if sums[i] is None else sums[i] + v

    for b, (i, j) in enumerate(PAIRS):
        v = packed[b * N : (b + 1) * N, :].astype(F32) * (1.0 / tokens)
        if i == j:
            v = jnp.where(eye, 0.0, v)
        a = jnp.abs(v)
        add(j, jnp.sum(a, axis=0, keepdims=True))
        if i != j:
            add(i, jnp.sum(a.T, axis=0, keepdims=True))
    sums = [s + jnp.abs(d) for s, d in zip(sums, diag)]
    factor = 1.0 / jnp.max(jnp.maximum(jnp.maximum(sums[0], sums[1]), sums[2]))
    d_row = [1.0 - factor * d for d in diag]
    d_col = [
        jnp.sum(jnp.where(eye, jnp.broadcast_to(d, (N, N)), 0.0), axis=1, keepdims=True)
        for d in d_row
    ]

    def put(ref, i, j, v):
        ref[i * N : (i + 1) * N, j * N : (j + 1) * N] = v.astype(BF16)
        if i != j:
            ref[j * N : (j + 1) * N, i * N : (i + 1) * N] = v.T.astype(BF16)

    scale = factor * (-1.0 / tokens)
    for b, (i, j) in enumerate(PAIRS):
        v = packed[b * N : (b + 1) * N, :].astype(F32) * scale
        if i == j:
            v = jnp.where(eye, 0.0, v)
        off_r[b] = v
        off_s[b] = v
        put(r_mat.at[0], i, j, v)
    s_row = [1.0 + d for d in d_row]
    s_col = [1.0 + d for d in d_col]

    def product(a, b, i, j):
        return jnp.dot(
            a[i * N : (i + 1) * N, :], b[:, j * N : (j + 1) * N], preferred_element_type=F32
        )

    def square(src, dst):
        for b, (i, j) in enumerate(PAIRS):
            v = off_r[b] * (d_col[i] + d_row[j]) + product(src, src, i, j)
            off_r[b] = v
            put(dst, i, j, v)

    square(r_mat.at[0], r_mat.at[1])
    d_row = [d * d for d in d_row]
    d_col = [d * d for d in d_col]
    now = 1
    left = r_mat.at[0]
    for k in range(4):
        last = k == 3
        for b, (i, j) in enumerate(PAIRS):
            v = s_col[i] * off_r[b] + off_s[b] * (1.0 + d_row[j])
            v = v + product(left, r_mat.at[now], i, j)
            if last:
                if i == j:
                    v = v + jnp.where(eye, s_row[j] * (1.0 + d_row[j]), 0.0)
                put(result, i, j, v * factor)
            else:
                off_s[b] = v
                put(s_mat.at[k % 2], i, j, v)
        if not last:
            s_row = [s * (1.0 + d) for s, d in zip(s_row, d_row)]
            s_col = [s * (1.0 + d) for s, d in zip(s_col, d_col)]
            left = s_mat.at[k % 2]
            square(r_mat.at[now], r_mat.at[3 - now])
            now = 3 - now
            d_row = [d * d for d in d_row]
            d_col = [d * d for d in d_col]


def kernel(
    tokens,
    damping,
    stats,
    grad,
    out,
    sbuf,
    partner_acc,
    own_acc,
    partner_in,
    y_out,
    y_in,
    packed,
    off_r,
    off_s,
    r_mat,
    s_mat,
    inverse,
    g_rows,
    g_buf,
    q_buf,
    o_buf,
    stats_sem,
    local_sem,
    grad_send,
    grad_recv,
    part_send,
    part_recv,
    y_send,
    y_recv,
    x_send,
    x_recv,
    g_send,
    g_recv,
    out_send,
    out_recv,
):
    dp = lax.axis_index("dp")
    o = lax.axis_index("owner")
    h, c = dp // 2, dp % 2
    x = o % 4
    quarter = W // 4
    half = W // 2

    def ring(t):
        return o - x + (x + t) % 4

    next_row = (o + 4) % 32
    prev_row = (o + 28) % 32
    partner = (h * 2 + 1 - c, o)
    across = ((1 - h) * 2 + c, o)

    loads = []
    steps = sbuf.shape[1] // TOKEN_CHUNK
    for j in range(2):
        f = (1 - c) if j == 0 else c
        for k in range(steps):
            rows = pl.ds(k * TOKEN_CHUNK, TOKEN_CHUNK)
            cp = pltpu.make_async_copy(
                stats.at[f, rows], sbuf.at[j, rows], stats_sem.at[j * steps + k]
            )
            cp.start()
            loads.append(cp)
    mine = pl.ds(pl.multiple_of(dp * quarter, quarter), quarter)
    local = []
    for tau in range(2):
        cp = pltpu.make_async_copy(grad.at[2 * c + tau], g_buf.at[tau, mine], local_sem.at[tau])
        cp.start()
        local.append(cp)

    barrier = pltpu.get_barrier_semaphore()

    def greet(device):
        pl.semaphore_signal(barrier, inc=1, device_id=device, device_id_type=MESH)

    greet(partner)
    greet(across)
    greet(((1 - h) * 2 + 1 - c, o))

    @pl.when(c == 0)
    def _():
        greet((dp, ring(1)))
        greet((dp, ring(3)))
        greet((dp + 1, ring(2)))
        greet((dp + 1, ring(3)))
        greet((dp, next_row))
        greet((dp, prev_row))
        pl.semaphore_wait(barrier, 9)

    @pl.when(c == 1)
    def _():
        greet((dp - 1, ring(2)))
        greet((dp - 1, ring(1)))
        pl.semaphore_wait(barrier, 5)

    def grad_copy(rel, tau):
        to_h = h if rel < 2 else 1 - h
        to_c = c if rel % 2 == 0 else 1 - c
        n = (rel - 1) * 2 + tau
        return pltpu.make_async_remote_copy(
            src_ref=grad.at[2 * to_c + tau],
            dst_ref=g_buf.at[tau, mine],
            send_sem=grad_send.at[n],
            recv_sem=grad_recv.at[n],
            device_id=(to_h * 2 + to_c, o),
            device_id_type=MESH,
        )

    grad_copy(2, 0).start()

    def partial(j, acc):
        for k in range(steps):
            loads[j * steps + k].wait()
            rows = slice(k * TOKEN_CHUNK, (k + 1) * TOKEN_CHUNK)
            for i in range(3):
                r = gram(sbuf[j, rows, i * N : (i + 1) * N], sbuf[j, rows, i * N :])
                for jj in range(i, 3):
                    b = PAIRS.index((i, jj))
                    v = r[:, (jj - i) * N : (jj - i + 1) * N]
                    if k == 0:
                        acc[b] = v
                    else:
                        acc[b] += v

    part_copies = [
        pltpu.make_async_remote_copy(
            src_ref=partner_acc.at[pl.ds(3 * k, 3)],
            dst_ref=partner_in.at[pl.ds(3 * k, 3)],
            send_sem=part_send.at[k],
            recv_sem=part_recv.at[k],
            device_id=partner,
            device_id_type=MESH,
        )
        for k in range(2)
    ]
    partial(0, partner_acc)
    for cp in part_copies:
        cp.start()
    partial(1, own_acc)

    grad_copy(1, 0).start()
    grad_copy(1, 1).start()

    eye = eye_mask()

    def y_copy(k):
        start, size = CHUNKS[k]
        return pltpu.make_async_remote_copy(
            src_ref=y_out.at[pl.ds(start, size)],
            dst_ref=y_in.at[pl.ds(start, size)],
            send_sem=y_send.at[k],
            recv_sem=y_recv.at[k],
            device_id=across,
            device_id_type=MESH,
        )

    diags = []
    for k in range(3):
        for b in CHUNK_PAIRS[k]:
            if b % 3 == 0:
                part_copies[b // 3].wait_recv()
            v = own_acc[b] + partner_in[b]
            own_acc[b] = v
            y_out[b * N : (b + 1) * N, :] = v.astype(BF16)
            if PAIRS[b][0] == PAIRS[b][1]:
                diags.append(jnp.sum(jnp.where(eye, v, 0.0), axis=0, keepdims=True))
        if k == 2:
            y_out[TAIL:ROWS, :] = pack_diagonal(diags)
        y_copy(k).start()

    def x_copy(t, k, slot):
        start, size = CHUNKS[k]
        to_slot = (2, 1, 1, 2)[t]
        device = (dp, next_row) if t == 0 else (dp + (0 if t == 1 else 1), ring(t))
        return pltpu.make_async_remote_copy(
            src_ref=packed.at[slot, pl.ds(start, size)],
            dst_ref=packed.at[to_slot, pl.ds(start, size)],
            send_sem=x_send.at[t * 3 + k],
            recv_sem=x_recv.at[to_slot * 3 + k],
            device_id=device,
            device_id_type=MESH,
        )

    lam = damping[c] * tokens
    for k in range(3):
        y_copy(k).wait_recv()
        for b in CHUNK_PAIRS[k]:
            rows = slice(b * N, (b + 1) * N)
            packed[0, rows, :] = (own_acc[b] + y_in[rows, :].astype(F32)).astype(BF16)
        if k == 2:
            other = unpack_diagonal(y_in[TAIL:ROWS, :])
            packed[0, TAIL:ROWS, :] = pack_diagonal([d + e + lam for d, e in zip(diags, other)])

        @pl.when((c == 0) & (x >= 1))
        def _():
            x_copy(0, k, 0).start()

        for t in range(1, 4):

            @pl.when((c == 0) & (x + t < 4))
            def _():
                x_copy(t, k, 0).start()

    for k in range(3):
        y_copy(k).wait_send()
    grad_copy(3, 0).start()
    grad_copy(2, 1).start()
    grad_copy(3, 1).start()

    @pl.when((c == 0) & (x >= 1))
    def _():
        for k in range(3):
            x_copy(0, k, 0).wait_recv()
            for t in range(1, 4):

                @pl.when(x + t >= 4)
                def _():
                    x_copy(t, k, 2).start()

    g_copy = pltpu.make_async_remote_copy(
        src_ref=g_rows,
        dst_ref=g_rows,
        send_sem=g_send.at[0],
        recv_sem=g_recv.at[0],
        device_id=partner,
        device_id_type=MESH,
    )
    chip_rows = pl.ds(pl.multiple_of(h * half, half), half)

    def one(n, _):
        @pl.when((c == 1) | (n < 2))
        def _():
            @pl.when(n == 1)
            def _():
                for k in range(3):
                    x_copy(1, k, 0).wait_recv()

            @pl.when(n == 2)
            def _():
                for k in range(3):
                    x_copy(3, k, 0).wait_recv()

            invert(packed.at[n], tokens, off_r, off_s, r_mat, s_mat, inverse.at[n])

            @pl.when((c == 1) & (n == 0))
            def _():
                g_rows[...] = inverse[0, chip_rows, :]
                g_copy.start()

        return 0

    lax.fori_loop(0, 3, one, 0)

    @pl.when(c == 0)
    def _():
        g_copy.wait_recv()

    own_rows = pl.ds(pl.multiple_of(c * quarter, quarter), quarter)
    other_rows = pl.ds(pl.multiple_of((1 - c) * quarter, quarter), quarter)

    def out_copy(tau):
        return pltpu.make_async_remote_copy(
            src_ref=o_buf.at[tau],
            dst_ref=out.at[2 * c + tau],
            send_sem=out_send.at[tau],
            recv_sem=out_recv.at[tau],
            device_id=partner,
            device_id_type=MESH,
        )

    for tau in range(2):
        local[tau].wait()
        for rel in (1, 2, 3):
            grad_copy(rel, tau).wait_recv()
        q_buf[...] = jnp.dot(g_rows[...], g_buf[tau], preferred_element_type=F32).astype(BF16)
        a = inverse.at[tau + c]
        o_buf[tau] = jnp.dot(q_buf[other_rows, :], a[...], preferred_element_type=F32).astype(BF16)
        out_copy(tau).start()
        out[2 * c + tau] = jnp.dot(q_buf[own_rows, :], a[...], preferred_element_type=F32).astype(
            BF16
        )

    for cp in part_copies:
        cp.wait_send()
    for rel in (1, 2, 3):
        for tau in range(2):
            grad_copy(rel, tau).wait_send()

    @pl.when(c == 1)
    def _():
        g_copy.wait_send()

    @pl.when(c == 0)
    def _():
        for k in range(3):

            @pl.when(x >= 1)
            def _():
                x_copy(0, k, 0).wait_send()

            for t in range(1, 4):
                x_copy(t, k, 0).wait_send()

    for tau in range(2):
        out_copy(tau).wait()


def per_device(stats, damping, grad, total_tokens):
    local_tokens = stats.shape[2]
    quarter, band, width = grad.shape[1:]
    tiles = jnp.swapaxes(grad[0], 0, 1)
    dma = pltpu.SemaphoreType.DMA
    import functools

    result = pl.pallas_call(
        functools.partial(kernel, float(total_tokens)),
        out_shape=jax.ShapeDtypeStruct((band, quarter, width), BF16),
        in_specs=[
            pl.BlockSpec(memory_space=pltpu.SMEM),
            pl.BlockSpec(memory_space=pl.ANY),
            pl.BlockSpec(memory_space=pl.ANY),
        ],
        out_specs=pl.BlockSpec(memory_space=pltpu.VMEM),
        scratch_shapes=[
            pltpu.VMEM((2, local_tokens, width), BF16),
            pltpu.VMEM((6, N, N), F32),
            pltpu.VMEM((6, N, N), F32),
            pltpu.VMEM((6, N, N), F32),
            pltpu.VMEM((ROWS, N), BF16),
            pltpu.VMEM((ROWS, N), BF16),
            pltpu.VMEM((3, ROWS, N), BF16),
            pltpu.VMEM((6, N, N), F32),
            pltpu.VMEM((6, N, N), F32),
            pltpu.VMEM((3, W, W), BF16),
            pltpu.VMEM((2, W, W), BF16),
            pltpu.VMEM((3, W, W), BF16),
            pltpu.VMEM((W // 2, W), BF16),
            pltpu.VMEM((2, W, W), BF16),
            pltpu.VMEM((W // 2, W), BF16),
            pltpu.VMEM((2, W // 4, W), BF16),
            dma((2 * local_tokens // TOKEN_CHUNK,)),
            dma((2,)),
            dma((6,)),
            dma((6,)),
            dma((2,)),
            dma((2,)),
            dma((3,)),
            dma((3,)),
            dma((12,)),
            dma((9,)),
            dma((1,)),
            dma((1,)),
            dma((2,)),
            dma((2,)),
        ],
        compiler_params=pltpu.CompilerParams(
            collective_id=0, has_side_effects=True, vmem_limit_bytes=56 * 2**20
        ),
    )(damping[0], stats[0], tiles)
    return jnp.swapaxes(result, 0, 1)[None]


def solution(mesh):
    in_specs = (P("owner", None, "dp", None), P("owner", None), P("owner", "dp", None, None))
    out_specs = P("owner", "dp", None, None)

    def whole(stats, damping, grad):
        def one(s, d, g):
            return per_device(s, d, g, stats.shape[2])

        return jax.shard_map(
            one, mesh=mesh, in_specs=in_specs, out_specs=out_specs, check_vma=False
        )(stats, damping, grad)

    return whole
```

time: 359 us -> 80.1 us (0.22)
  waiting for transfers between devices: 246 us -> 0 us
  matrix products: 81.7 us -> 0 us
  Pallas kernels: 0 us -> 74.3 us
  between operations: 14.2 us -> 0.01 us
  starting transfers between devices: 5.12 us -> 0 us
  other arithmetic: 4.41 us -> 0 us
    psum x1 -> x0, waiting for transfers between devices: 104 us -> none  [per_device(): summed = lax.psum(partial_cov, 'dp')]
    dot_general x16 -> x0, matrix products: 81.7 us -> none  [the longest x5 35.8 us: per_device(): jnp.dot(matrix, iterate, precision=HIGH, preferred_element_type=jnp.float32)]
    ppermute x3 -> x0, waiting for transfers between devices: 75.5 us -> none  [passed_along(): return lax.ppermute(block, axis, route)]
    pallas_call x0 -> x1, Pallas kernels: none -> 74.3 us  [per_device(): pl.pallas_call(functools.partial(kernel, float(total_tokens)), out_shape=...]
    all_gather x2 -> x0, waiting for transfers between devices: 65.7 us -> none  [the longest x1 38.1 us: per_device(): lax.all_gather(right_flat, 'dp', axis=0, tiled=True)]
    ppermute x3 -> x0, starting transfers between devices: 4.86 us -> none  [passed_along(): return lax.ppermute(block, axis, route)]
  transfers between devices with their start and end apart: 6 -> 0, of which waited for: 6 -> 0; matrix products, arithmetic and copies ran while one was open for 1% -> 0% of each run, Pallas kernels for 0% -> 0%
where the time goes in v1:
time: 80.1 us; the launch traced here: 79.9 us
  Pallas kernels  74.3 us (93%)
  local copies, waits for them, and re-layouts  5.6 us (7%)
    pallas_call x1, Pallas kernels, per_device(): pl.pallas_call(functools.partial(kernel, float(total_tokens)), out_shape=...  74.3 us
    broadcast_in_dim x1, local copies, waits for them, and re-layouts, per_device(): return jnp.swapaxes(result, 0, 1)[None]  3.2 us
    unnamed x1, local copies, waits for them, and re-layouts  2.4 us

profile of v1, /device:TPU:1, one launch (start us, length us, event | category | flops | bytes accessed | tf_op | source)
XLA Modules:
  0.0 79.9 jit_solution(16884927741695390020)
XLA Ops:
  0.0 2.4 %copy.7 = bf16[1,192,4,768]{3,1,2,0:T(8,128)(2,1)} copy(bf16[1,192,4,768]{3,2,1,0:T(4,128)(2,1)} %param.5) | data formatting | bytes 2359296 | tf_op args[2]
  2.4 74.3 %shard_map.37 = bf16[4,192,768]{2,1,0:T(8,128)(2,1)} custom-call(f32[2]{0:T(128)} %bitcast.13, bf16[2,2048,768]{2,1,0:T(8,128)(2,1)} %bitcast.10, bf16[4,192,768]{2,1,0:T(8,128)(2,1)} %bitcast.12), custom_call_target="tpu_custom_call" | custom-call | tf_op jit(solution)/shard_map/pallas_call | solution.py:437
  76.7 3.2 %copy.5 = bf16[1,192,4,768]{3,2,1,0:T(4,128)(2,1)} copy(bf16[1,192,4,768]{3,1,2,0:T(8,128)(2,1)} %bitcast.11) | data formatting | bytes 2359296 | tf_op jit(solution)/shard_map/broadcast_in_dim | solution.py:482

commit v2 on v1

v2 whole, which is shorter than its diff:
```python
import functools

import jax
import jax.numpy as jnp
from jax import lax
from jax.experimental import pallas as pl
from jax.experimental.pallas import tpu as pltpu
from jax.sharding import PartitionSpec as P

MESH = pl.DeviceIdType.MESH
F32 = jnp.float32
BF16 = jnp.bfloat16
N = 256
W = 768
PAIRS = ((0, 0), (0, 1), (0, 2), (1, 1), (1, 2), (2, 2))
H = N // 2
OFF = {(0, 1): 0, (0, 2): N, (1, 2): 2 * N}
UPPER = 3 * N
LOWER = UPPER + 3 * H
TAIL = LOWER + H + H // 2
ROWS = TAIL + 16
CHUNKS = tuple((k * N, N if k < 5 else ROWS - 5 * N) for k in range(6))
DATA = tuple((k * N, N if k < 5 else TAIL - 5 * N) for k in range(6))
TOKEN_CHUNK = 1024


def eye_mask():
    shape = (N, N)
    return lax.broadcasted_iota(jnp.int32, shape, 0) == lax.broadcasted_iota(jnp.int32, shape, 1)


def gram(a, b):
    return lax.dot_general(a, b, (((0,), (0,)), ((), ())), preferred_element_type=F32)


def pack_diagonal(diags):
    row = lax.broadcasted_iota(jnp.int32, (16, N), 0)
    out = jnp.zeros((16, N), F32)
    for i, d in enumerate(diags):
        high = d.astype(BF16).astype(F32)
        out = jnp.where(row == i, high, out)
        out = jnp.where(row == i + 5, d - high, out)
    return out.astype(BF16)


def unpack_diagonal(tail):
    t = tail.astype(F32)
    return [t[i : i + 1] + t[i + 5 : i + 6] for i in range(5)]


def add_block(acc, f, i, j, v, first):
    def put(rows, columns, w):
        if first:
            acc[f, rows, columns] = w
        else:
            acc[f, rows, columns] += w

    full = slice(0, N)
    if i != j:
        put(slice(OFF[i, j], OFF[i, j] + N), full, v)
        return
    put(slice(UPPER + i * H, UPPER + (i + 1) * H), full, v[:H])
    low = v[H:, H:]
    if i < 2:
        put(slice(LOWER, LOWER + H), slice(i * H, (i + 1) * H), low)
    else:
        rows = slice(LOWER + H, TAIL)
        put(rows, slice(0, H), low[: H // 2])
        put(rows, slice(H, N), low[H // 2 :])


def diagonals(k, v, bias):
    def pick(w, mask):
        return jnp.sum(jnp.where(mask, w + bias, 0.0), axis=0, keepdims=True)

    row = lax.broadcasted_iota(jnp.int32, (H, N), 0)
    lane = lax.broadcasted_iota(jnp.int32, (H, N), 1)
    if k == 3:
        return [pick(v[:H], row == lane), pick(v[H:], row == lane)]
    if k == 4:
        return [pick(v[:H], row == lane), pick(v[H:], row == lane % H)]
    if k == 5:
        row, lane = row[: H // 2], lane[: H // 2]
        return [pick(v, (lane == row) | (lane == row + H + H // 2))]
    return []


def invert(packed, tokens, off_r, off_s, r_mat, s_mat, result):
    eye = eye_mask()
    parts = [d * (1.0 / tokens) for d in unpack_diagonal(packed[TAIL:ROWS, :])]
    seconds = [parts[3][:, :H], parts[3][:, H:], parts[4][:, :H] + parts[4][:, H:]]
    diag = [jnp.concatenate([parts[i][:, :H], seconds[i]], axis=1) for i in range(3)]
    sums = [None] * 3

    def add(i, v):
        sums[i] = v if sums[i] is None else sums[i] + v

    def unpack(i, j):
        if i != j:
            return packed[OFF[i, j] : OFF[i, j] + N, :].astype(F32)
        top = packed[UPPER + i * H : UPPER + (i + 1) * H, :].astype(F32)
        if i < 2:
            low = packed[LOWER : LOWER + H, i * H : (i + 1) * H].astype(F32)
        else:
            both = packed[LOWER + H : TAIL, :].astype(F32)
            low = jnp.concatenate([both[:, :H], both[:, H:]], axis=0)
        bottom = jnp.concatenate([top[:, H:].T, low], axis=1)
        return jnp.concatenate([top, bottom], axis=0)

    for b, (i, j) in enumerate(PAIRS):
        v = unpack(i, j) * (1.0 / tokens)
        if i == j:
            v = jnp.where(eye, 0.0, v)
        off_r[b] = v
        a = jnp.abs(v)
        add(j, jnp.sum(a, axis=0, keepdims=True))
        if i != j:
            add(i, jnp.sum(a.T, axis=0, keepdims=True))
    sums = [s + jnp.abs(d) for s, d in zip(sums, diag)]
    factor = 1.0 / jnp.max(jnp.maximum(jnp.maximum(sums[0], sums[1]), sums[2]))
    d_row = [1.0 - factor * d for d in diag]
    d_col = [
        jnp.sum(jnp.where(eye, jnp.broadcast_to(d, (N, N)), 0.0), axis=1, keepdims=True)
        for d in d_row
    ]

    def put(ref, i, j, v):
        ref[i * N : (i + 1) * N, j * N : (j + 1) * N] = v.astype(BF16)
        if i != j:
            ref[j * N : (j + 1) * N, i * N : (i + 1) * N] = v.T.astype(BF16)

    for b, (i, j) in enumerate(PAIRS):
        v = off_r[b] * (-factor)
        off_r[b] = v
        off_s[b] = v
        put(r_mat.at[0], i, j, v)
    s_row = [1.0 + d for d in d_row]
    s_col = [1.0 + d for d in d_col]

    def product(a, b, i, j):
        return jnp.dot(
            a[i * N : (i + 1) * N, :], b[:, j * N : (j + 1) * N], preferred_element_type=F32
        )

    def square(src, dst):
        for b, (i, j) in enumerate(PAIRS):
            v = off_r[b] * (d_col[i] + d_row[j]) + product(src, src, i, j)
            off_r[b] = v
            put(dst, i, j, v)

    square(r_mat.at[0], r_mat.at[1])
    d_row = [d * d for d in d_row]
    d_col = [d * d for d in d_col]
    now = 1
    left = r_mat.at[0]
    for k in range(4):
        last = k == 3
        for b, (i, j) in enumerate(PAIRS):
            v = s_col[i] * off_r[b] + off_s[b] * (1.0 + d_row[j])
            v = v + product(left, r_mat.at[now], i, j)
            if last:
                if i == j:
                    v = v + jnp.where(eye, s_row[j] * (1.0 + d_row[j]), 0.0)
                put(result, i, j, v * factor)
            else:
                off_s[b] = v
                put(s_mat.at[k % 2], i, j, v)
        if not last:
            s_row = [s * (1.0 + d) for s, d in zip(s_row, d_row)]
            s_col = [s * (1.0 + d) for s, d in zip(s_col, d_col)]
            left = s_mat.at[k % 2]
            square(r_mat.at[now], r_mat.at[3 - now])
            now = 3 - now
            d_row = [d * d for d in d_row]
            d_col = [d * d for d in d_col]


def kernel(
    tokens,
    damping,
    stats,
    grad,
    out,
    sbuf,
    native,
    tiles,
    acc,
    partner_in,
    y_out,
    y_in,
    z_out,
    packed,
    off_r,
    off_s,
    r_mat,
    s_mat,
    inverse,
    g_rows,
    g_buf,
    q_buf,
    o_buf,
    o_all,
    stats_sem,
    local_sem,
    grad_send,
    grad_recv,
    part_send,
    part_recv,
    y_send,
    y_recv,
    z_send,
    x_send,
    x_recv,
    m_send,
    g_send,
    g_recv,
    out_send,
    out_recv,
    go,
):
    dp = lax.axis_index("dp")
    o = lax.axis_index("owner")
    h, c = dp // 2, dp % 2
    x, l, z = o % 4, (o // 4) % 2, o // 8
    quarter = W // 4
    half = W // 2

    def ring(t):
        return o - x + (x + t) % 4

    def y_place(step):
        y = (h * 2 + l + step) % 4
        return (y // 2) * 2 + c, z * 8 + (y % 2) * 4 + x

    def z_place(step):
        return dp, (o + 8 * step) % 32

    partner = (h * 2 + 1 - c, o)
    across = ((1 - h) * 2 + c, o)

    steps = sbuf.shape[1] // TOKEN_CHUNK

    def load(f, k):
        rows = pl.ds(k * TOKEN_CHUNK, TOKEN_CHUNK)
        return pltpu.make_async_copy(
            stats.at[f, rows], sbuf.at[f, rows], stats_sem.at[f * steps + k]
        )

    tiles_load = pltpu.make_async_copy(grad, native, local_sem.at[2])
    tiles_load.start()
    for f in range(2):
        for k in range(steps):
            load(f, k).start()
    mine = pl.ds(pl.multiple_of(dp * quarter, quarter), quarter)

    def own_tile(tau):
        return pltpu.make_async_copy(
            tiles.at[2 * c + tau], g_buf.at[tau, mine], local_sem.at[tau]
        )

    barrier = pltpu.get_barrier_semaphore()

    def greet(device):
        pl.semaphore_signal(barrier, inc=1, device_id=device, device_id_type=MESH)

    greet(partner)
    greet(across)
    greet(((1 - h) * 2 + 1 - c, o))

    @pl.when(c == 0)
    def _():
        greet((dp, ring(1)))
        greet((dp, ring(3)))
        greet((dp + 1, ring(2)))
        greet((dp + 1, ring(3)))
        for step in (1, 3):
            greet(y_place(step))
            greet(z_place(step))

    @pl.when(c == 1)
    def _():
        greet((dp - 1, ring(2)))
        greet((dp - 1, ring(1)))

    tiles_load.wait()
    tiles[...] = jnp.swapaxes(native[...], 0, 1)

    @pl.when(c == 0)
    def _():
        pl.semaphore_wait(barrier, 11)

    @pl.when(c == 1)
    def _():
        pl.semaphore_wait(barrier, 5)

    def grad_copy(rel, tau):
        to_h = h if rel < 2 else 1 - h
        to_c = c if rel % 2 == 0 else 1 - c
        n = (rel - 1) * 2 + tau
        return pltpu.make_async_remote_copy(
            src_ref=tiles.at[2 * to_c + tau],
            dst_ref=g_buf.at[tau, mine],
            send_sem=grad_send.at[n],
            recv_sem=grad_recv.at[n],
            device_id=(to_h * 2 + to_c, o),
            device_id_type=MESH,
        )

    def send_later_grads():
        grad_copy(3, 0).start()
        grad_copy(2, 1).start()
        grad_copy(3, 1).start()

    grad_copy(2, 0).start()
    for tau in range(2):
        own_tile(tau).start()

    def part_copy(k):
        rows = pl.ds(0, UPPER) if k == 0 else pl.ds(UPPER, TAIL - UPPER)
        return pltpu.make_async_remote_copy(
            src_ref=acc.at[1 - c, rows],
            dst_ref=partner_in.at[rows],
            send_sem=part_send.at[k],
            recv_sem=part_recv.at[k],
            device_id=partner,
            device_id_type=MESH,
        )

    def partial(f, _):
        for k in range(steps):
            load(f, k).wait()
            rows = slice(k * TOKEN_CHUNK, (k + 1) * TOKEN_CHUNK)
            for i in range(3):
                r = gram(sbuf[f, rows, i * N : (i + 1) * N], sbuf[f, rows, i * N :])
                for j in range(i, 3):
                    add_block(acc, f, i, j, r[:, (j - i) * N : (j - i + 1) * N], k == 0)

        @pl.when(f == 1 - c)
        def _():
            for k in range(2):
                part_copy(k).start()

        return 0

    lax.fori_loop(0, 2, partial, 0)
    grad_copy(1, 0).start()
    grad_copy(1, 1).start()
    bias = damping[c] * (0.5 * tokens)

    def sum_of_chip(k, diags):
        if k % 3 == 0:
            part_copy(k // 3).wait_recv()
        start, size = DATA[k]
        rows = slice(start, start + size)
        v = acc[c, rows, :] + partner_in[rows, :]
        acc[c, rows, :] = v
        y_out[rows, :] = v.astype(BF16)
        diags.extend(diagonals(k, v, bias))
        if k == 5:
            y_out[TAIL:ROWS, :] = pack_diagonal(diags)

    def y_copy(src, slot, device, k, send):
        start, size = CHUNKS[k]
        return pltpu.make_async_remote_copy(
            src_ref=src.at[pl.ds(start, size)],
            dst_ref=y_in.at[slot, pl.ds(start, size)],
            send_sem=y_send.at[send],
            recv_sem=y_recv.at[slot * 6 + k],
            device_id=device,
            device_id_type=MESH,
        )

    def y_plus(k):
        return y_copy(y_out, 0, y_place(1), k, k)

    def y_minus(k):
        return y_copy(y_out, 1, y_place(3), k, 6 + k)

    def y_on(k):
        if k < 3:
            return y_copy(y_in.at[0], 2, y_place(1), k, 12 + k)
        return y_copy(y_in.at[1], 2, y_place(3), k, 12 + k)

    def y_across(k):
        return y_copy(y_out, 2, across, k, k)

    def x_copy(t, k, slot):
        start, size = CHUNKS[k]
        to_slot = (1, 1, 2)[t - 1]
        return pltpu.make_async_remote_copy(
            src_ref=packed.at[slot, pl.ds(start, size)],
            dst_ref=packed.at[to_slot, pl.ds(start, size)],
            send_sem=x_send.at[(t - 1) * 6 + k],
            recv_sem=x_recv.at[to_slot * 6 + k],
            device_id=(dp + (0 if t == 1 else 1), ring(t)),
            device_id_type=MESH,
        )

    def z_copy(k):
        start, size = CHUNKS[k]
        return pltpu.make_async_remote_copy(
            src_ref=z_out.at[pl.ds(start, size)],
            dst_ref=packed.at[3, pl.ds(start, size)],
            send_sem=z_send.at[k],
            recv_sem=x_recv.at[18 + k],
            device_id=z_place(1),
            device_id_type=MESH,
        )

    def m_copy(k):
        start, size = CHUNKS[k]
        return pltpu.make_async_remote_copy(
            src_ref=packed.at[0, pl.ds(start, size)],
            dst_ref=packed.at[2, pl.ds(start, size)],
            send_sem=m_send.at[k],
            recv_sem=x_recv.at[12 + k],
            device_id=partner,
            device_id_type=MESH,
        )

    def sum_of_row(k, diags):
        start, size = DATA[k]
        rows = slice(start, start + size)
        packed[0, rows, :] = (acc[c, rows, :] + y_in[2, rows, :].astype(F32)).astype(BF16)
        if k == 5:
            other = unpack_diagonal(y_in[2, TAIL:ROWS, :])
            packed[0, TAIL:ROWS, :] = pack_diagonal([d + e for d, e in zip(diags, other)])

    def sum_of_other_row(k, dst):
        start, size = DATA[k]
        rows = slice(start, start + size)
        dst[rows, :] = (y_in[0, rows, :].astype(F32) + y_in[1, rows, :].astype(F32)).astype(BF16)
        if k == 5:
            one = unpack_diagonal(y_in[0, TAIL:ROWS, :])
            two = unpack_diagonal(y_in[1, TAIL:ROWS, :])
            dst[TAIL:ROWS, :] = pack_diagonal([d + e for d, e in zip(one, two)])

    def send_on(k, slot, ts):
        for t in ts:

            @pl.when((x + t < 4) if slot == 0 else (x + t >= 4))
            def _():
                x_copy(t, k, slot).start()

    @pl.when(c == 0)
    def _():
        diags = []
        for k in range(6):
            sum_of_chip(k, diags)
            if k < 3:
                y_plus(k).start()
            if k < 4:
                y_minus(k).start()

        def other_row(k):
            @pl.when(l == 0)
            def _():
                sum_of_other_row(k, z_out)
                z_copy(k).start()

            @pl.when(l == 1)
            def _():
                sum_of_other_row(k, packed.at[3])
                send_on(k, 3, (1, 2, 3))

        def from_z(k):
            @pl.when(l == 0)
            def _():
                z_copy(k).wait_recv()
                send_on(k, 3, (1, 2, 3))

        def own_row(k):
            y_on(k).wait_recv()
            sum_of_row(k, diags)
            send_on(k, 0, (1, 2, 3))

        for k in range(3):
            y_plus(k).wait_recv()
            y_on(k).start()
            y_plus(k + 3).start()
            y_minus(k).wait_recv()
            other_row(k)
            if k >= 2:
                from_z(k - 2)
        for k in range(3, 6):
            y_minus(k).wait_recv()
            y_on(k).start()
            if k < 5:
                y_minus(k + 1).start()
            else:
                pl.semaphore_signal(go, inc=1, device_id=partner, device_id_type=MESH)
            y_plus(k).wait_recv()
            other_row(k)
            from_z(k - 2)
            if k == 4:
                own_row(0)
        own_row(3)
        own_row(1)
        from_z(4)
        own_row(4)
        own_row(2)
        from_z(5)
        own_row(5)
        send_later_grads()
    @pl.when(c == 1)
    def _():
        diags = []
        for k in range(6):
            sum_of_chip(k, diags)
        pl.semaphore_wait(go, 1)
        for k in range(6):
            y_across(k).start()
        for k in range(6):
            y_across(k).wait_recv()
            sum_of_row(k, diags)
            m_copy(k).start()
        send_later_grads()

    g_copy = pltpu.make_async_remote_copy(
        src_ref=g_rows,
        dst_ref=g_rows,
        send_sem=g_send.at[0],
        recv_sem=g_recv.at[0],
        device_id=partner,
        device_id_type=MESH,
    )
    chip_rows = pl.ds(pl.multiple_of(h * half, half), half)

    def one(n, _):
        slot = (1 - c) * ((2 * n) % 3) + c * ((n + 1) % 3)

        @pl.when((c == 0) | (n < 2))
        def _():
            @pl.when(slot >= 1)
            def _():
                for k in range(6):
                    start, size = CHUNKS[k]
                    pltpu.make_async_remote_copy(
                        src_ref=packed.at[0, pl.ds(start, size)],
                        dst_ref=packed.at[1, pl.ds(start, size)],
                        send_sem=m_send.at[k],
                        recv_sem=x_recv.at[slot * 6 + k],
                        device_id=partner,
                        device_id_type=MESH,
                    ).wait_recv()

            invert(packed.at[slot], tokens, off_r, off_s, r_mat, s_mat, inverse.at[slot])

            @pl.when((c == 0) & (n == 1))
            def _():
                g_rows[...] = inverse[2, chip_rows, :]
                g_copy.start()

        return 0

    lax.fori_loop(0, 3, one, 0)

    @pl.when(c == 1)
    def _():
        g_copy.wait_recv()

    own_rows = pl.ds(pl.multiple_of(c * quarter, quarter), quarter)
    other_rows = pl.ds(pl.multiple_of((1 - c) * quarter, quarter), quarter)

    def out_copy(tau):
        return pltpu.make_async_remote_copy(
            src_ref=o_buf.at[tau],
            dst_ref=o_all.at[2 * c + tau],
            send_sem=out_send.at[tau],
            recv_sem=out_recv.at[tau],
            device_id=partner,
            device_id_type=MESH,
        )

    def tile(tau, _):
        own_tile(tau).wait()
        for rel in (1, 2, 3):
            grad_copy(rel, tau).wait_recv()
        q_buf[...] = jnp.dot(g_rows[...], g_buf[tau], preferred_element_type=F32).astype(BF16)
        a = inverse.at[tau + c]
        o_buf[tau] = jnp.dot(q_buf[other_rows, :], a[...], preferred_element_type=F32).astype(BF16)
        out_copy(tau).start()
        o_all[2 * c + tau] = jnp.dot(q_buf[own_rows, :], a[...], preferred_element_type=F32).astype(
            BF16
        )
        return 0

    lax.fori_loop(0, 2, tile, 0)

    for k in range(2):
        part_copy(k).wait_send()
    for rel in (1, 2, 3):
        for tau in range(2):
            grad_copy(rel, tau).wait_send()

    @pl.when(c == 1)
    def _():
        for k in range(6):
            y_across(k).wait_send()
            m_copy(k).wait_send()

    @pl.when(c == 0)
    def _():
        g_copy.wait_send()
        for k in range(6):
            y_plus(k).wait_send()
            y_minus(k).wait_send()
            y_on(k).wait_send()

            @pl.when(l == 0)
            def _():
                z_copy(k).wait_send()

            for t in range(1, 4):
                x_copy(t, k, 0).wait_send()

    for tau in range(2):
        out_copy(tau).wait()
    out[...] = jnp.swapaxes(o_all[...], 0, 1)


def per_device(stats, damping, grad, total_tokens):
    local_tokens = stats.shape[2]
    quarter, band, width = grad.shape[1:]
    dma = pltpu.SemaphoreType.DMA
    result = pl.pallas_call(
        functools.partial(kernel, float(total_tokens)),
        out_shape=jax.ShapeDtypeStruct((quarter, band, width), BF16),
        in_specs=[
            pl.BlockSpec(memory_space=pltpu.SMEM),
            pl.BlockSpec(memory_space=pl.ANY),
            pl.BlockSpec(memory_space=pl.ANY),
        ],
        out_specs=pl.BlockSpec(memory_space=pltpu.VMEM),
        scratch_shapes=[
            pltpu.VMEM((2, local_tokens, width), BF16),
            pltpu.VMEM((quarter, band, width), BF16),
            pltpu.VMEM((band, quarter, width), BF16),
            pltpu.VMEM((2, TAIL, N), F32),
            pltpu.VMEM((TAIL, N), F32),
            pltpu.VMEM((ROWS, N), BF16),
            pltpu.VMEM((3, ROWS, N), BF16),
            pltpu.VMEM((ROWS, N), BF16),
            pltpu.VMEM((4, ROWS, N), BF16),
            pltpu.VMEM((6, N, N), F32),
            pltpu.VMEM((6, N, N), F32),
            pltpu.VMEM((3, W, W), BF16),
            pltpu.VMEM((2, W, W), BF16),
            pltpu.VMEM((3, W, W), BF16),
            pltpu.VMEM((W // 2, W), BF16),
            pltpu.VMEM((2, W, W), BF16),
            pltpu.VMEM((W // 2, W), BF16),
            pltpu.VMEM((2, W // 4, W), BF16),
            pltpu.VMEM((band, quarter, width), BF16),
            dma((2 * local_tokens // TOKEN_CHUNK,)),
            dma((3,)),
            dma((6,)),
            dma((6,)),
            dma((2,)),
            dma((2,)),
            dma((18,)),
            dma((18,)),
            dma((6,)),
            dma((18,)),
            dma((24,)),
            dma((6,)),
            dma((1,)),
            dma((1,)),
            dma((2,)),
            dma((2,)),
            pltpu.SemaphoreType.REGULAR,
        ],
        compiler_params=pltpu.CompilerParams(
            collective_id=0, has_side_effects=True, vmem_limit_bytes=56 * 2**20
        ),
    )(damping[0], stats[0], grad[0])
    return result[None]


def solution(mesh):
    in_specs = (P("owner", None, "dp", None), P("owner", None), P("owner", "dp", None, None))
    out_specs = P("owner", "dp", None, None)

    def whole(stats, damping, grad):
        def one(s, d, g):
            return per_device(s, d, g, stats.shape[2])

        return jax.shard_map(
            one, mesh=mesh, in_specs=in_specs, out_specs=out_specs, check_vma=False
        )(stats, damping, grad)

    return whole
```

time: 80.1 us -> 73.4 us (0.916)
  Pallas kernels: 74.3 us -> 70.6 us
  local copies, waits for them, and re-layouts: 5.6 us -> 2.69 us
    pallas_call x1, Pallas kernels: 74.3 us -> 70.6 us  [per_device(): pl.pallas_call(functools.partial(kernel, float(total_tokens)), out_shape=...]
    broadcast_in_dim x1 -> x0, local copies, waits for them, and re-layouts: 3.2 us -> none  [per_device(): return jnp.swapaxes(result, 0, 1)[None]]
where the time goes in v2:
time: 73.4 us; the launch traced here: 73.3 us
  Pallas kernels  70.6 us (96%)
  local copies, waits for them, and re-layouts  2.69 us (4%)
    pallas_call x1, Pallas kernels, per_device(): pl.pallas_call(functools.partial(kernel, float(total_tokens)), out_shape=...  70.6 us
    unnamed x1, local copies, waits for them, and re-layouts  2.69 us

profile of v2, /device:TPU:1, one launch (start us, length us, event | category | flops | bytes accessed | tf_op | source)
XLA Modules:
  0.0 73.3 jit_solution(2090623199942682566)
XLA Ops:
  0.0 70.6 %shard_map.37 = bf16[192,4,768]{2,1,0:T(4,128)(2,1)} custom-call(f32[2]{0:T(128)} %bitcast.7, bf16[2,2048,768]{2,1,0:T(8,128)(2,1)} %bitcast.4, bf16[192,4,768]{2,1,0:T(4,128)(2,1)} %bitcast.6), custom_call_target="tpu_custom_call" | custom-call | tf_op jit(solution)/shard_map/pallas_call | solution.py:626
  70.6 2.7 %copy.5 = bf16[1,192,4,768]{3,2,1,0:T(4,128)(2,1)} copy(bf16[1,192,4,768]{3,2,1,0:T(4,128)(2,1)} %bitcast.5) | data formatting | bytes 2359296

commit v3 on v2

--- a/solution.py
+++ b/solution.py
@@ -180,7 +180,7 @@
     damping,
     stats,
     grad,
-    out,
+    o_all,
     sbuf,
     native,
     tiles,
@@ -199,7 +199,6 @@
     g_buf,
     q_buf,
     o_buf,
-    o_all,
     stats_sem,
     local_sem,
     grad_send,
@@ -487,7 +486,7 @@
             y_on(k).start()
             if k < 5:
                 y_minus(k + 1).start()
-            else:
+            if k == 4:
                 pl.semaphore_signal(go, inc=1, device_id=partner, device_id_type=MESH)
             y_plus(k).wait_recv()
             other_row(k)
@@ -616,7 +615,10 @@
 
     for tau in range(2):
         out_copy(tau).wait()
-    out[...] = jnp.swapaxes(o_all[...], 0, 1)
+
+
+def rows_first(by_tile, out):
+    out[...] = jnp.swapaxes(by_tile[...], 0, 1)
 
 
 def per_device(stats, damping, grad, total_tokens):
@@ -625,7 +627,7 @@
     dma = pltpu.SemaphoreType.DMA
     result = pl.pallas_call(
         functools.partial(kernel, float(total_tokens)),
-        out_shape=jax.ShapeDtypeStruct((quarter, band, width), BF16),
+        out_shape=jax.ShapeDtypeStruct((band, quarter, width), BF16),
         in_specs=[
             pl.BlockSpec(memory_space=pltpu.SMEM),
             pl.BlockSpec(memory_space=pl.ANY),
@@ -651,7 +653,6 @@
             pltpu.VMEM((2, W, W), BF16),
             pltpu.VMEM((W // 2, W), BF16),
             pltpu.VMEM((2, W // 4, W), BF16),
-            pltpu.VMEM((band, quarter, width), BF16),
             dma((2 * local_tokens // TOKEN_CHUNK,)),
             dma((3,)),
             dma((6,)),
@@ -674,7 +675,12 @@
             collective_id=0, has_side_effects=True, vmem_limit_bytes=56 * 2**20
         ),
     )(damping[0], stats[0], grad[0])
-    return result[None]
+    return pl.pallas_call(
+        rows_first,
+        out_shape=jax.ShapeDtypeStruct((quarter, band, width), BF16),
+        in_specs=[pl.BlockSpec(memory_space=pltpu.VMEM)],
+        out_specs=pl.BlockSpec(memory_space=pltpu.VMEM),
+    )(result)[None]
 
 
 def solution(mesh):

time: 73.4 us -> 70.3 us (0.958); the launches traced: 73.3 us -> 69.2 us
  local copies, waits for them, and re-layouts: 2.69 us -> 0 us
  Pallas kernels: 70.6 us -> 69.2 us
    pallas_call x1, Pallas kernels: 70.6 us -> 66.4 us  [per_device(): pl.pallas_call(functools.partial(kernel, float(total_tokens)), out_shape=...]
    pallas_call x0 -> x1, Pallas kernels: none -> 2.78 us  [per_device(): pl.pallas_call(rows_first, out_shape=jax.ShapeDtypeStruct((quarter, band,...]
    unnamed x1 -> x0, local copies, waits for them, and re-layouts: 2.69 us -> none
where the time goes in v3:
time: 70.3 us; the launch traced here: 69.2 us
  Pallas kernels  69.2 us (98%)
    pallas_call x1, Pallas kernels, per_device(): pl.pallas_call(functools.partial(kernel, float(total_tokens)), out_shape=...  66.4 us
    pallas_call x1, Pallas kernels, per_device(): pl.pallas_call(rows_first, out_shape=jax.ShapeDtypeStruct((quarter, band,...  2.78 us

profile of v3, /device:TPU:1, one launch (start us, length us, event | category | flops | bytes accessed | tf_op | source)
XLA Modules:
  0.0 69.2 jit_solution(6923724856822253603)
XLA Ops:
  0.0 66.4 %shard_map.37.by_tile = bf16[4,192,768]{2,1,0:T(8,128)(2,1)} custom-call(f32[2]{0:T(128)} %bitcast.6, bf16[2,2048,768]{2,1,0:T(8,128)(2,1)} %bitcast.4, bf16[192,4,768]{2,1,0:T(4,128)(2,1)} %bitcast.5), custom_call_target="tpu_custom_call" | custom-call | tf_op jit(solution)/shard_map/pallas_call | solution.py:628
  66.4 2.8 %shard_map.38 = bf16[192,4,768]{2,1,0:T(4,128)(2,1)} custom-call(bf16[4,192,768]{2,1,0:T(8,128)(2,1)} %shard_map.37.by_tile), custom_call_target="tpu_custom_call" | custom-call | tf_op jit(solution)/shard_map/pallas_call | solution.py:678

commit v4 on v3

--- a/solution.py
+++ b/solution.py
@@ -198,6 +198,7 @@
     g_rows,
     g_buf,
     q_buf,
+    q_sum,
     o_buf,
     stats_sem,
     local_sem,
@@ -524,6 +525,7 @@
         device_id_type=MESH,
     )
     chip_rows = pl.ds(pl.multiple_of(h * half, half), half)
+    far_rows = pl.ds(pl.multiple_of((1 - h) * half, half), half)
 
     def one(n, _):
         slot = (1 - c) * ((2 * n) % 3) + c * ((n + 1) % 3)
@@ -573,9 +575,16 @@
 
     def tile(tau, _):
         own_tile(tau).wait()
-        for rel in (1, 2, 3):
+        grad_copy(1, tau).wait_recv()
+        q_sum[...] = jnp.dot(
+            g_rows[:, chip_rows], g_buf[tau, chip_rows, :], preferred_element_type=F32
+        )
+        for rel in (2, 3):
             grad_copy(rel, tau).wait_recv()
-        q_buf[...] = jnp.dot(g_rows[...], g_buf[tau], preferred_element_type=F32).astype(BF16)
+        rest = jnp.dot(
+            g_rows[:, far_rows], g_buf[tau, far_rows, :], preferred_element_type=F32
+        )
+        q_buf[...] = (q_sum[...] + rest).astype(BF16)
         a = inverse.at[tau + c]
         o_buf[tau] = jnp.dot(q_buf[other_rows, :], a[...], preferred_element_type=F32).astype(BF16)
         out_copy(tau).start()
@@ -652,6 +661,7 @@
             pltpu.VMEM((W // 2, W), BF16),
             pltpu.VMEM((2, W, W), BF16),
             pltpu.VMEM((W // 2, W), BF16),
+            pltpu.VMEM((W // 2, W), F32),
             pltpu.VMEM((2, W // 4, W), BF16),
             dma((2 * local_tokens // TOKEN_CHUNK,)),
             dma((3,)),

time: 70.3 us -> 70.9 us (level)
  no operation moved by 1% of the time
where the time goes in v4:
time: 70.9 us; the launch traced here: 69.8 us
  Pallas kernels  69.8 us (98%)
    pallas_call x1, Pallas kernels, per_device(): pl.pallas_call(functools.partial(kernel, float(total_tokens)), out_shape=...  67 us
    pallas_call x1, Pallas kernels, per_device(): pl.pallas_call(rows_first, out_shape=jax.ShapeDtypeStruct((quarter, band,...  2.78 us

profile of v4, /device:TPU:1, one launch (start us, length us, event | category | flops | bytes accessed | tf_op | source)
XLA Modules:
  0.0 69.8 jit_solution(11653116353397838092)
XLA Ops:
  0.0 67.0 %shard_map.37.by_tile = bf16[4,192,768]{2,1,0:T(8,128)(2,1)} custom-call(f32[2]{0:T(128)} %bitcast.6, bf16[2,2048,768]{2,1,0:T(8,128)(2,1)} %bitcast.4, bf16[192,4,768]{2,1,0:T(4,128)(2,1)} %bitcast.5), custom_call_target="tpu_custom_call" | custom-call | tf_op jit(solution)/shard_map/pallas_call | solution.py:637
  67.0 2.8 %shard_map.38 = bf16[192,4,768]{2,1,0:T(4,128)(2,1)} custom-call(bf16[4,192,768]{2,1,0:T(8,128)(2,1)} %shard_map.37.by_tile), custom_call_target="tpu_custom_call" | custom-call | tf_op jit(solution)/shard_map/pallas_call | solution.py:688
